TPU v7x, 1024 devices: a whole 4x8x16 slice. The times are simulated.
1024 devices in a mesh: row: 128 (over y, z), task: 8 (over x, core).
Axes of the slice: x: 4, y: 8, z: 16, core: 2. Of those that a mesh axis runs over, the one named last changes fastest.
Arguments:
- a_vals: float32 [8192, 8, 4096], P('row', 'task'), may hold values from -0.75 to 0.75
- a_cols: int32 [8192, 8], P('row', 'task'), may hold values from 0 to 8191, as said below
- a_len: int32 [8192], P('row'), may hold values from 1 to 8, as said below
- p_vals: float32 [8192, 2, 4096], P('row'), may hold values from -0.75 to 0.75
- p_cols: int32 [8192, 2], P('row'), may hold values from 0 to 1023, as said below
Outputs:
- c_tiles: float32 [1024, 7, 4096], P(('row', 'task'))
Inputs may be any that keep to these rules, and one draw needn't show every extreme that they name: `a_cols`: slot 0 of fine block-row i holds i itself; the 8 columns of a row are distinct and lie in a window of 13 block-rows, i - 6 to i + 6, moved inside 0 to 8191 at the two ends. The live slots of a row are its first a_len ones; the first fine block-row of every slab of 64 has all 8 live and the last has one. `p_cols`: the two entries of fine block-row i are distinct, each one of i // 8 - 1, i // 8, i // 8 + 1.
All inputs are finite; a program needn't handle non-finite values.
Results may differ from a plain program's by a relative error of at most 0.0003.
Values sent between devices are 32-bit elements; how exact they have to be, the bound alone decides.
A program may use at most 128 MiB of HBM per device.

v0:
```python
import functools

import jax
import jax.numpy as jnp
from jax import lax
from jax.experimental import pallas as pl
from jax.experimental.pallas import tpu as pltpu
from jax.sharding import PartitionSpec as P

TILE = 64
RATIO = 8
FW = 6
SLAB = 64
HALF = 32
MESH = pl.DeviceIdType.MESH
F32 = jnp.float32
BF16 = jnp.bfloat16


def split(x):
    high = x.astype(BF16)
    low = (x - high.astype(F32)).astype(BF16)
    return high, low


def kernel(
    row_count,
    a_hbm,
    acol_any,
    p_hbm,
    pcol_any,
    acol,
    alen,
    pcol,
    out_ref,
    a_own,
    a_sib,
    p_raw,
    p_halo,
    acol_sib_v,
    pcol_halo_v,
    acol_sib,
    pcol_halo,
    band_high,
    band_low,
    left,
    ap_high,
    ap_low,
    sums,
    flat,
    sib_out,
    sib_in,
    edge_out,
    edge_in,
    gathered,
    a_local_sem,
    a_send_sem,
    a_recv_sem,
    p_local_sem,
    halo_send_sem,
    halo_recv_sem,
    int_send_sem,
    int_recv_sem,
    int_local_sem,
    cross_send_sem,
    cross_recv_sem,
    sum_send_sem,
    sum_recv_sem,
):
    row = lax.axis_index("row")
    task = lax.axis_index("task")
    core = task % 2
    chip = task // 2
    other = task + 1 - 2 * core
    beside = (row + row_count + 2 * core - 1) % row_count
    sib_id = (row, other)
    edge_id = (beside, other)

    barrier = pltpu.get_barrier_semaphore()
    for step in range(1, 8):
        pl.semaphore_signal(barrier, inc=1, device_id=(row, (task + step) % 8), device_id_type=MESH)
    pl.semaphore_signal(barrier, inc=1, device_id=edge_id, device_id_type=MESH)

    def home_of(u, which):
        return 3 - u + which * (1 + 2 * u)

    p_copies = []
    for u in (-1, 0, 1, 2, 3):
        first = 32 - 6 * core if u < 0 else 8 * home_of(u, core)
        size = 6 if u < 0 else 8
        copy = pltpu.make_async_copy(
            p_hbm.at[pl.ds(first, size)], p_raw.at[pl.ds(first - 26 * core, size)], p_local_sem.at[u + 1]
        )
        copy.start()
        p_copies.append(copy)
    a_copies = []
    for u in range(4):
        copy = pltpu.make_async_copy(
            a_hbm.at[pl.ds(8 * home_of(u, core), 8)], a_own.at[pl.ds(8 * u, 8)], a_local_sem.at[u]
        )
        copy.start()
        a_copies.append(copy)

    pl.semaphore_wait(barrier, 8)

    acol_copy = pltpu.make_async_remote_copy(
        acol_any, acol_sib_v, int_send_sem.at[0], int_recv_sem.at[0], device_id=sib_id, device_id_type=MESH
    )
    acol_copy.start()
    pcol_copy = pltpu.make_async_remote_copy(
        pcol_any, pcol_halo_v, int_send_sem.at[1], int_recv_sem.at[1], device_id=edge_id, device_id_type=MESH
    )
    pcol_copy.start()
    halo_copy = pltpu.make_async_remote_copy(
        p_hbm.at[pl.ds(58 * core, FW)], p_halo, halo_send_sem, halo_recv_sem, device_id=edge_id, device_id_type=MESH
    )
    halo_copy.start()
    a_sends = []
    for u in range(4):
        copy = pltpu.make_async_remote_copy(
            a_hbm.at[pl.ds(8 * home_of(u, 1 - core), 8)],
            a_sib.at[pl.ds(8 * u, 8)],
            a_send_sem.at[u],
            a_recv_sem.at[u],
            device_id=sib_id,
            device_id_type=MESH,
        )
        copy.start()
        a_sends.append(copy)

    lane = lax.broadcasted_iota(jnp.int32, (HALF, 128), 1)
    lower = lane < TILE
    upper_bit = lane // TILE
    parity_order = upper_bit * TILE + 2 * (lane % HALF) + (lane % TILE) // HALF

    def put_band(tiles, index, offset0, offset1, u_parity):
        x0 = tiles[0]
        x1 = tiles[1]
        r0 = pltpu.roll(x0, TILE, 1)
        r1 = pltpu.roll(x1, TILE, 1)
        even0, odd0 = jnp.where(lower, x0, r0), jnp.where(lower, r0, x0)
        even1, odd1 = jnp.where(lower, x1, r1), jnp.where(lower, r1, x1)
        place0 = offset0 + 1 - u_parity
        place1 = offset1 + 1 - u_parity
        for pair in range(2):
            here = upper_bit + 2 * pair
            take0 = here == place0
            take1 = here == place1
            for part, y0, y1 in ((0, even0, even1), (1, odd0, odd1)):
                high, low = split(jnp.where(take0, y0, jnp.where(take1, y1, 0.0)))
                band_high[index, pl.ds(HALF * part, HALF), pl.ds(128 * pair, 128)] = high
                band_low[index, pl.ds(HALF * part, HALF), pl.ds(128 * pair, 128)] = low

    def offset_of(column, home):
        offset = column - home + 1
        return 2 - offset + core * (2 * offset - 2)

    def prepare(u):
        count = 8 if 0 <= u < 4 else FW
        parity = u % 2

        def one(k, carry):
            if u == 4:
                v = 37 - k + core * (2 * k - 5)
                home = 8 * row - 1 + 9 * core
                at = k + 58 * (1 - core)
                tiles = [p_halo[k, pl.ds(which, HALF, stride=2), :] for which in range(2)]
                offsets = [offset_of(pcol_halo[which, at], home) for which in range(2)]
            else:
                j = (32 - 6 * core if u < 0 else 8 * home_of(u, core)) + k
                v = 31 - j + core * (2 * j - 63)
                home = 8 * row + (4 - core if u < 0 else home_of(u, core))
                tiles = [p_raw[j - 26 * core, pl.ds(which, HALF, stride=2), :] for which in range(2)]
                offsets = [offset_of(pcol[which, j], home) for which in range(2)]
            put_band(tiles, v + FW, offsets[0], offsets[1], parity)
            if 0 <= u < 4:
                for d in range(3):
                    zero = jnp.zeros_like(lane)
                    picked = jnp.where(
                        zero + offsets[0] == d, tiles[0], jnp.where(zero + offsets[1] == d, tiles[1], 0.0)
                    )
                    left[u, d, k // 4, pl.ds(HALF * (k % 4), HALF), :] = picked
            return carry

        lax.fori_loop(0, count, one, 0, unroll=2)

    def products(u):
        home = home_of(u, core)

        def one(k, carry):
            j = 8 * home + k
            length = alen[j]
            zero = jnp.zeros((TILE, 128), jnp.int32)
            total = [0.0, 0.0, 0.0]
            for tiles, columns, slot in ((a_own, acol, task), (a_sib, acol_sib, other)):
                column = columns[0, j] - SLAB * row
                v = jnp.clip(31 - column + core * (2 * column - 63), -FW, HALF + FW - 1)
                live = jnp.where(slot < length, 1.0, 0.0).astype(F32)
                raw = tiles[8 * u + k] * live
                near = jnp.take_along_axis(raw, parity_order, axis=1)
                far = pltpu.roll(near, TILE, 1)
                twice = jnp.concatenate([jnp.where(lower, near, far), jnp.where(lower, far, near)], axis=0)
                high, low = split(twice)
                tile = jnp.concatenate([high, low[:, :TILE]], axis=1)
                right_high = band_high[v + FW]
                right_low = band_low[v + FW]
                right = jnp.concatenate([right_high, right_low, right_high], axis=0)
                product = jnp.dot(tile, right, preferred_element_type=F32)
                first, second = product[:, :128], product[:, 128:]
                shift = ((v + 8) // 8 - 2 + 4) // 2 - (u - 2 + 4) // 2
                still = zero + shift == 0
                total[0] = total[0] + jnp.where(still, first, 0.0)
                total[1] = total[1] + jnp.where(still, second, first)
                total[2] = total[2] + jnp.where(still, 0.0, second)
            at = 256 * (k // 4) + HALF * (k % 4)
            for pair in range(3):
                high, low = split(total[pair])
                for part in range(2):
                    place = pl.ds(pl.multiple_of(at + 128 * part, HALF), HALF)
                    lanes = pl.ds(128 * pair, 128)
                    ap_high[place, lanes] = high[HALF * part : HALF * (part + 1)]
                    ap_low[place, lanes] = low[HALF * part : HALF * (part + 1)]
            return carry

        lax.fori_loop(0, 8, one, 0, unroll=2)

    def coarse(u):
        high_parts, low_parts = [], []
        for d in range(3):
            high_row, low_row = [], []
            for group in range(2):
                high, low = split(left[u, d, group].T)
                high_row += [high[:TILE], high[TILE:]]
                low_row += [low[:TILE], low[TILE:]]
            high_parts.append(jnp.concatenate(high_row, axis=1))
            low_parts.append(jnp.concatenate(low_row, axis=1))
        high = jnp.concatenate(high_parts, axis=0)
        low = jnp.concatenate(low_parts, axis=0)
        result = jnp.dot(high, ap_high[...], preferred_element_type=F32)
        result = result + jnp.dot(high, ap_low[...], preferred_element_type=F32)
        result = result + jnp.dot(low, ap_high[...], preferred_element_type=F32)
        for d in range(3):
            begin = (1, 1 - u % 2, 0)[d]
            fresh = d == 2 or u == 0
            for pair in range(4):
                inside = begin <= pair < begin + 3
                if inside:
                    value = result[TILE * d : TILE * (d + 1), 128 * (pair - begin) : 128 * (pair - begin + 1)]
                    if fresh:
                        sums[u + d, pair] = value
                    else:
                        sums[u + d, pair] += value
                elif fresh:
                    sums[u + d, pair] = jnp.zeros((TILE, 128), F32)

    def flatten(w, deltas, target, correction):
        for delta in deltas:
            place = w + delta
            pair = place // 2 - (w - 3) // 2
            even = sums[w + 1, pair, pl.ds(0, HALF, stride=2), :]
            odd = sums[w + 1, pair, pl.ds(1, HALF, stride=2), :]
            if place % 2 == 0:
                value = jnp.where(lower, even, pltpu.roll(odd, TILE, 1))
            else:
                value = jnp.where(lower, pltpu.roll(even, TILE, 1), odd)
            target[3 + (2 * core - 1) * delta - correction] = value

    mine = core == chip // 2

    def sum_copy(w):
        owner = home_of(w, core)
        copy = pltpu.make_async_remote_copy(
            flat.at[w],
            gathered.at[chip],
            sum_send_sem.at[w],
            sum_recv_sem.at[chip],
            device_id=(row, owner),
            device_id_type=MESH,
        )
        return copy, owner == task

    def send_sum(w):
        copy, local = sum_copy(w)

        @pl.when(local)
        def _():
            gathered[chip] = flat[w]

        @pl.when(jnp.logical_not(local))
        def _():
            copy.start()

    sib_copy = pltpu.make_async_remote_copy(
        sib_out, sib_in, cross_send_sem.at[0], cross_recv_sem.at[0], device_id=sib_id, device_id_type=MESH
    )
    edge_copy = pltpu.make_async_remote_copy(
        edge_out, edge_in, cross_send_sem.at[1], cross_recv_sem.at[1], device_id=edge_id, device_id_type=MESH
    )
    everything = range(-3, 4)

    p_copies[0].wait()
    prepare(-1)
    p_copies[1].wait()
    prepare(0)
    p_copies[2].wait()
    prepare(1)
    acol_copy.wait()
    to_smem = pltpu.make_async_copy(acol_sib_v, acol_sib, int_local_sem.at[0])
    to_smem.start()
    to_smem.wait()
    for u in range(4):
        a_copies[u].wait()
        a_sends[u].wait()
        products(u)
        coarse(u)
        if u == 0:
            flatten(-1, range(-1, 4), sib_out, 2 * core)
            sib_copy.start()
            p_copies[3].wait()
            prepare(2)
        elif u == 1:
            flatten(0, everything, flat.at[0], 0)
            sib_copy.wait()
            begin = 2 - 2 * core
            for k in range(5):
                flat[0, begin + k] += sib_in[k]
            send_sum(0)
            p_copies[4].wait()
            prepare(3)
        elif u == 2:
            flatten(1, everything, flat.at[1], 0)
            send_sum(1)
            halo_copy.wait()
            pcol_copy.wait()
            to_smem = pltpu.make_async_copy(pcol_halo_v, pcol_halo, int_local_sem.at[1])
            to_smem.start()
            to_smem.wait()
            prepare(4)
        else:
            flatten(4, range(-3, 2), edge_out, 2 - 2 * core)
            edge_copy.start()
            flatten(2, everything, flat.at[2], 0)
            send_sum(2)
            flatten(3, everything, flat.at[3], 0)
            edge_copy.wait()
            begin = 2 * core
            for k in range(5):
                flat[3, begin + k] += edge_in[k]
            send_sum(3)

    for w in range(4):
        copy, local = sum_copy(w)

        @pl.when(jnp.logical_not(local))
        def _():
            copy.wait_send()

    for source in range(4):
        copy = pltpu.make_async_remote_copy(
            flat.at[0],
            gathered.at[source],
            sum_send_sem.at[0],
            sum_recv_sem.at[source],
            device_id=(row, other),
            device_id_type=MESH,
        )

        @pl.when(jnp.logical_not(jnp.logical_and(mine, chip == source)))
        def _():
            copy.wait_recv()

    out_ref[...] = (gathered[0] + gathered[1]) + (gathered[2] + gathered[3])


def on_device(row_count, a_vals, a_cols, a_len, p_vals, p_cols):
    a_tiles = a_vals.reshape(SLAB, HALF, 128)
    p_tiles = p_vals.reshape(SLAB, 2, HALF, 128).transpose(0, 2, 1, 3).reshape(SLAB, TILE, 128)
    acol = a_cols.reshape(1, SLAB)
    pcol = p_cols.T
    alen = a_len
    dma = pltpu.SemaphoreType.DMA
    smem = pl.BlockSpec(memory_space=pltpu.SMEM)
    anywhere = pl.BlockSpec(memory_space=pl.ANY)
    out = pl.pallas_call(
        functools.partial(kernel, row_count),
        out_shape=jax.ShapeDtypeStruct((7, HALF, 128), F32),
        in_specs=[anywhere, anywhere, anywhere, anywhere, smem, smem, smem],
        out_specs=pl.BlockSpec(memory_space=pltpu.VMEM),
        scratch_shapes=[
            pltpu.VMEM((HALF, HALF, 128), F32),
            pltpu.VMEM((HALF, HALF, 128), F32),
            pltpu.VMEM((38, TILE, 128), F32),
            pltpu.VMEM((FW, TILE, 128), F32),
            pltpu.VMEM((1, SLAB), jnp.int32),
            pltpu.VMEM((2, SLAB), jnp.int32),
            pltpu.SMEM((1, SLAB), jnp.int32),
            pltpu.SMEM((2, SLAB), jnp.int32),
            pltpu.VMEM((44, TILE, 256), BF16),
            pltpu.VMEM((44, TILE, 256), BF16),
            pltpu.VMEM((4, 3, 2, 128, 128), F32),
            pltpu.VMEM((512, 384), BF16),
            pltpu.VMEM((512, 384), BF16),
            pltpu.VMEM((6, 4, TILE, 128), F32),
            pltpu.VMEM((4, 7, HALF, 128), F32),
            pltpu.VMEM((5, HALF, 128), F32),
            pltpu.VMEM((5, HALF, 128), F32),
            pltpu.VMEM((5, HALF, 128), F32),
            pltpu.VMEM((5, HALF, 128), F32),
            pltpu.VMEM((4, 7, HALF, 128), F32),
            dma((4,)),
            dma((4,)),
            dma((4,)),
            dma((5,)),
            dma,
            dma,
            dma((2,)),
            dma((2,)),
            dma((2,)),
            dma((2,)),
            dma((2,)),
            dma((4,)),
            dma((4,)),
        ],
        compiler_params=pltpu.CompilerParams(
            collective_id=0, has_side_effects=True, vmem_limit_bytes=60 * 1024 * 1024
        ),
        name="triple_product",
    )(a_tiles, acol, p_tiles, pcol, acol, alen, pcol)
    return out.reshape(1, 7, TILE * TILE)


def solution(mesh):
    in_specs = (
        P("row", "task", None),
        P("row", "task"),
        P("row"),
        P("row", None, None),
        P("row", None),
    )
    out_specs = P(("row", "task"), None, None)
    return jax.shard_map(
        functools.partial(on_device, mesh.shape["row"]),
        mesh=mesh,
        in_specs=in_specs,
        out_specs=out_specs,
        check_vma=False,
    )
```

profile of v0, /device:TPU:48, one launch (start us, length us, event | category | flops | bytes accessed | tf_op | source)
XLA Modules:
  0.0 42.4 jit_solution(6391825584771291873)
XLA Ops:
  0.0 40.8 %triple_product.1 = f32[7,32,128]{2,1,0:T(8,128)} custom-call(f32[64,32,128]{2,1,0:T(8,128)} %bitcast.10, s32[1,64]{1,0:T(1,128)} %bitcast.14, f32[64,64,128]{2,1,0:T(8,128)} %bitcast.9, s32[2,64]{1,0:T(2,128)} %bitcast.12, s32[1,64]{1,0:T(1,128)} %bitcast.15, s32[64]{0:T(128)} %alen.1, s32[2,64]{1,0:T(2,128)} %bitcast.13), custom_call_target="tpu_custom_call" | custom-call | tf_op jit(solution)/shard_map/triple_product/pallas_call | solution.py:384
  40.8 1.6 %copy.11 = f32[1,7,4096]{2,0,1:T(1,128)} copy(f32[1,7,4096]{2,0,1:T(1,128)} %bitcast.11) | data formatting | bytes 229376
where the time goes:
time: 42.5 us; the launch traced here: 42.4 us
  Pallas kernels  40.8 us (96%)
  local copies, waits for them, and re-layouts  1.55 us (4%)
    pallas_call x1, Pallas kernels, on_device(): pl.pallas_call(functools.partial(kernel, row_count), out_shape=jax.ShapeD...  40.8 us
    unnamed x1, local copies, waits for them, and re-layouts  1.55 us

commit v1 on v0

--- a/solution.py
+++ b/solution.py
@@ -73,13 +73,17 @@
     chip = task // 2
     other = task + 1 - 2 * core
     beside = (row + row_count + 2 * core - 1) % row_count
+    has_edge = jnp.logical_or(jnp.logical_and(core == 0, row > 0), jnp.logical_and(core == 1, row < row_count - 1))
     sib_id = (row, other)
     edge_id = (beside, other)
 
     barrier = pltpu.get_barrier_semaphore()
     for step in range(1, 8):
         pl.semaphore_signal(barrier, inc=1, device_id=(row, (task + step) % 8), device_id_type=MESH)
-    pl.semaphore_signal(barrier, inc=1, device_id=edge_id, device_id_type=MESH)
+
+    @pl.when(has_edge)
+    def _():
+        pl.semaphore_signal(barrier, inc=1, device_id=edge_id, device_id_type=MESH)
 
     def home_of(u, which):
         return 3 - u + which * (1 + 2 * u)
@@ -101,7 +105,7 @@
         copy.start()
         a_copies.append(copy)
 
-    pl.semaphore_wait(barrier, 8)
+    pl.semaphore_wait(barrier, jnp.where(has_edge, 8, 7))
 
     acol_copy = pltpu.make_async_remote_copy(
         acol_any, acol_sib_v, int_send_sem.at[0], int_recv_sem.at[0], device_id=sib_id, device_id_type=MESH
@@ -110,11 +114,15 @@
     pcol_copy = pltpu.make_async_remote_copy(
         pcol_any, pcol_halo_v, int_send_sem.at[1], int_recv_sem.at[1], device_id=edge_id, device_id_type=MESH
     )
-    pcol_copy.start()
     halo_copy = pltpu.make_async_remote_copy(
         p_hbm.at[pl.ds(58 * core, FW)], p_halo, halo_send_sem, halo_recv_sem, device_id=edge_id, device_id_type=MESH
     )
-    halo_copy.start()
+
+    @pl.when(has_edge)
+    def _():
+        pcol_copy.start()
+        halo_copy.start()
+
     a_sends = []
     for u in range(4):
         copy = pltpu.make_async_remote_copy(
@@ -330,22 +338,34 @@
         elif u == 2:
             flatten(1, everything, flat.at[1], 0)
             send_sum(1)
-            halo_copy.wait()
-            pcol_copy.wait()
-            to_smem = pltpu.make_async_copy(pcol_halo_v, pcol_halo, int_local_sem.at[1])
-            to_smem.start()
-            to_smem.wait()
-            prepare(4)
+
+            @pl.when(has_edge)
+            def _():
+                halo_copy.wait()
+                pcol_copy.wait()
+                to_smem = pltpu.make_async_copy(pcol_halo_v, pcol_halo, int_local_sem.at[1])
+                to_smem.start()
+                to_smem.wait()
+                prepare(4)
+
         else:
-            flatten(4, range(-3, 2), edge_out, 2 - 2 * core)
-            edge_copy.start()
+
+            @pl.when(has_edge)
+            def _():
+                flatten(4, range(-3, 2), edge_out, 2 - 2 * core)
+                edge_copy.start()
+
             flatten(2, everything, flat.at[2], 0)
             send_sum(2)
             flatten(3, everything, flat.at[3], 0)
-            edge_copy.wait()
-            begin = 2 * core
-            for k in range(5):
-                flat[3, begin + k] += edge_in[k]
+
+            @pl.when(has_edge)
+            def _():
+                edge_copy.wait()
+                begin = 2 * core
+                for k in range(5):
+                    flat[3, begin + k] += edge_in[k]
+
             send_sum(3)
 
     for w in range(4):

time: 42.5 us -> 42.6 us (level)
  the two profiles are of different devices: /device:TPU:48 before, /device:TPU:40 now
where the time goes in v1:
time: 42.6 us; the launch traced here: 42.4 us
  Pallas kernels  40.8 us (96%)
  local copies, waits for them, and re-layouts  1.55 us (4%)
    pallas_call x1, Pallas kernels, on_device(): pl.pallas_call(functools.partial(kernel, row_count), out_shape=jax.ShapeD...  40.8 us
    unnamed x1, local copies, waits for them, and re-layouts  1.55 us

profile of v1, /device:TPU:40, one launch (start us, length us, event | category | flops | bytes accessed | tf_op | source)
XLA Modules:
  0.0 42.4 jit_solution(6247261181606845685)
XLA Ops:
  0.0 40.8 %triple_product.1 = f32[7,32,128]{2,1,0:T(8,128)} custom-call(f32[64,32,128]{2,1,0:T(8,128)} %bitcast.10, s32[1,64]{1,0:T(1,128)} %bitcast.14, f32[64,64,128]{2,1,0:T(8,128)} %bitcast.9, s32[2,64]{1,0:T(2,128)} %bitcast.12, s32[1,64]{1,0:T(1,128)} %bitcast.15, s32[64]{0:T(128)} %alen.1, s32[2,64]{1,0:T(2,128)} %bitcast.13), custom_call_target="tpu_custom_call" | custom-call | tf_op jit(solution)/shard_map/triple_product/pallas_call | solution.py:404
  40.8 1.6 %copy.11 = f32[1,7,4096]{2,0,1:T(1,128)} copy(f32[1,7,4096]{2,0,1:T(1,128)} %bitcast.11) | data formatting | bytes 229376

commit v2 on v0

--- a/solution.py
+++ b/solution.py
@@ -29,9 +29,7 @@
     acol_any,
     p_hbm,
     pcol_any,
-    acol,
-    alen,
-    pcol,
+    alen_any,
     out_ref,
     a_own,
     a_sib,
@@ -62,6 +60,9 @@
     int_send_sem,
     int_recv_sem,
     int_local_sem,
+    acol,
+    alen,
+    pcol,
     cross_send_sem,
     cross_recv_sem,
     sum_send_sem,
@@ -73,16 +74,26 @@
     chip = task // 2
     other = task + 1 - 2 * core
     beside = (row + row_count + 2 * core - 1) % row_count
+    has_edge = jnp.logical_or(jnp.logical_and(core == 0, row > 0), jnp.logical_and(core == 1, row < row_count - 1))
     sib_id = (row, other)
     edge_id = (beside, other)
 
     barrier = pltpu.get_barrier_semaphore()
     for step in range(1, 8):
         pl.semaphore_signal(barrier, inc=1, device_id=(row, (task + step) % 8), device_id_type=MESH)
-    pl.semaphore_signal(barrier, inc=1, device_id=edge_id, device_id_type=MESH)
+
+    @pl.when(has_edge)
+    def _():
+        pl.semaphore_signal(barrier, inc=1, device_id=edge_id, device_id_type=MESH)
 
     def home_of(u, which):
         return 3 - u + which * (1 + 2 * u)
+
+    int_copies = []
+    for k, (source, target) in enumerate(((acol_any, acol), (alen_any, alen), (pcol_any, pcol))):
+        copy = pltpu.make_async_copy(source, target, int_local_sem.at[2 + k])
+        copy.start()
+        int_copies.append(copy)
 
     p_copies = []
     for u in (-1, 0, 1, 2, 3):
@@ -101,7 +112,7 @@
         copy.start()
         a_copies.append(copy)
 
-    pl.semaphore_wait(barrier, 8)
+    pl.semaphore_wait(barrier, jnp.where(has_edge, 8, 7))
 
     acol_copy = pltpu.make_async_remote_copy(
         acol_any, acol_sib_v, int_send_sem.at[0], int_recv_sem.at[0], device_id=sib_id, device_id_type=MESH
@@ -110,11 +121,15 @@
     pcol_copy = pltpu.make_async_remote_copy(
         pcol_any, pcol_halo_v, int_send_sem.at[1], int_recv_sem.at[1], device_id=edge_id, device_id_type=MESH
     )
-    pcol_copy.start()
     halo_copy = pltpu.make_async_remote_copy(
         p_hbm.at[pl.ds(58 * core, FW)], p_halo, halo_send_sem, halo_recv_sem, device_id=edge_id, device_id_type=MESH
     )
-    halo_copy.start()
+
+    @pl.when(has_edge)
+    def _():
+        pcol_copy.start()
+        halo_copy.start()
+
     a_sends = []
     for u in range(4):
         copy = pltpu.make_async_remote_copy(
@@ -128,6 +143,7 @@
         copy.start()
         a_sends.append(copy)
 
+    sums[...] = jnp.zeros_like(sums)
     lane = lax.broadcasted_iota(jnp.int32, (HALF, 128), 1)
     lower = lane < TILE
     upper_bit = lane // TILE
@@ -182,7 +198,7 @@
                     left[u, d, k // 4, pl.ds(HALF * (k % 4), HALF), :] = picked
             return carry
 
-        lax.fori_loop(0, count, one, 0, unroll=2)
+        lax.fori_loop(0, count, one, 0, unroll=True)
 
     def products(u):
         home = home_of(u, core)
@@ -222,7 +238,7 @@
                     ap_low[place, lanes] = low[HALF * part : HALF * (part + 1)]
             return carry
 
-        lax.fori_loop(0, 8, one, 0, unroll=2)
+        lax.fori_loop(0, 8, one, 0, unroll=True)
 
     def coarse(u):
         high_parts, low_parts = [], []
@@ -241,17 +257,8 @@
         result = result + jnp.dot(low, ap_high[...], preferred_element_type=F32)
         for d in range(3):
             begin = (1, 1 - u % 2, 0)[d]
-            fresh = d == 2 or u == 0
-            for pair in range(4):
-                inside = begin <= pair < begin + 3
-                if inside:
-                    value = result[TILE * d : TILE * (d + 1), 128 * (pair - begin) : 128 * (pair - begin + 1)]
-                    if fresh:
-                        sums[u + d, pair] = value
-                    else:
-                        sums[u + d, pair] += value
-                elif fresh:
-                    sums[u + d, pair] = jnp.zeros((TILE, 128), F32)
+            for pair in range(3):
+                sums[u + d, pair + begin] += result[TILE * d : TILE * (d + 1), 128 * pair : 128 * (pair + 1)]
 
     def flatten(w, deltas, target, correction):
         for delta in deltas:
@@ -298,55 +305,77 @@
     )
     everything = range(-3, 4)
 
+    def work(u):
+        a_copies[u].wait()
+        a_sends[u].wait()
+        products(u)
+        coarse(u)
+
+    for copy in int_copies:
+        copy.wait()
     p_copies[0].wait()
     prepare(-1)
-    p_copies[1].wait()
-    prepare(0)
-    p_copies[2].wait()
-    prepare(1)
+    for u in range(4):
+        p_copies[u + 1].wait()
+        prepare(u)
     acol_copy.wait()
     to_smem = pltpu.make_async_copy(acol_sib_v, acol_sib, int_local_sem.at[0])
     to_smem.start()
     to_smem.wait()
-    for u in range(4):
-        a_copies[u].wait()
-        a_sends[u].wait()
-        products(u)
-        coarse(u)
-        if u == 0:
-            flatten(-1, range(-1, 4), sib_out, 2 * core)
-            sib_copy.start()
-            p_copies[3].wait()
-            prepare(2)
-        elif u == 1:
-            flatten(0, everything, flat.at[0], 0)
-            sib_copy.wait()
-            begin = 2 - 2 * core
-            for k in range(5):
-                flat[0, begin + k] += sib_in[k]
-            send_sum(0)
-            p_copies[4].wait()
-            prepare(3)
-        elif u == 2:
-            flatten(1, everything, flat.at[1], 0)
-            send_sum(1)
-            halo_copy.wait()
+
+    def edge_home():
+        @pl.when(has_edge)
+        def _():
             pcol_copy.wait()
             to_smem = pltpu.make_async_copy(pcol_halo_v, pcol_halo, int_local_sem.at[1])
             to_smem.start()
             to_smem.wait()
+            halo_copy.wait()
             prepare(4)
-        else:
+
+        work(3)
+
+        @pl.when(has_edge)
+        def _():
             flatten(4, range(-3, 2), edge_out, 2 - 2 * core)
             edge_copy.start()
-            flatten(2, everything, flat.at[2], 0)
-            send_sum(2)
-            flatten(3, everything, flat.at[3], 0)
-            edge_copy.wait()
-            begin = 2 * core
-            for k in range(5):
-                flat[3, begin + k] += edge_in[k]
-            send_sum(3)
+
+    work(0)
+    flatten(-1, range(-1, 4), sib_out, 2 * core)
+    sib_copy.start()
+
+    @pl.when(core == 1)
+    def _():
+        edge_home()
+
+    work(1)
+    flatten(0, everything, flat.at[0], 0)
+    sib_copy.wait()
+    begin = 2 - 2 * core
+    for k in range(5):
+        flat[0, begin + k] += sib_in[k]
+    send_sum(0)
+
+    work(2)
+    flatten(1, everything, flat.at[1], 0)
+    send_sum(1)
+
+    @pl.when(core == 0)
+    def _():
+        edge_home()
+
+    flatten(2, everything, flat.at[2], 0)
+    send_sum(2)
+    flatten(3, everything, flat.at[3], 0)
+
+    @pl.when(has_edge)
+    def _():
+        edge_copy.wait()
+        begin = 2 * core
+        for k in range(5):
+            flat[3, begin + k] += edge_in[k]
+
+    send_sum(3)
 
     for w in range(4):
         copy, local = sum_copy(w)
@@ -379,12 +408,11 @@
     pcol = p_cols.T
     alen = a_len
     dma = pltpu.SemaphoreType.DMA
-    smem = pl.BlockSpec(memory_space=pltpu.SMEM)
     anywhere = pl.BlockSpec(memory_space=pl.ANY)
     out = pl.pallas_call(
         functools.partial(kernel, row_count),
         out_shape=jax.ShapeDtypeStruct((7, HALF, 128), F32),
-        in_specs=[anywhere, anywhere, anywhere, anywhere, smem, smem, smem],
+        in_specs=[anywhere, anywhere, anywhere, anywhere, anywhere],
         out_specs=pl.BlockSpec(memory_space=pltpu.VMEM),
         scratch_shapes=[
             pltpu.VMEM((HALF, HALF, 128), F32),
@@ -415,7 +443,10 @@
             dma,
             dma((2,)),
             dma((2,)),
-            dma((2,)),
+            dma((5,)),
+            pltpu.SMEM((1, SLAB), jnp.int32),
+            pltpu.SMEM((SLAB,), jnp.int32),
+            pltpu.SMEM((2, SLAB), jnp.int32),
             dma((2,)),
             dma((2,)),
             dma((4,)),
@@ -425,7 +456,7 @@
             collective_id=0, has_side_effects=True, vmem_limit_bytes=60 * 1024 * 1024
         ),
         name="triple_product",
-    )(a_tiles, acol, p_tiles, pcol, acol, alen, pcol)
+    )(a_tiles, acol, p_tiles, pcol, alen)
     return out.reshape(1, 7, TILE * TILE)
 
 

time: 42.5 us -> 38.1 us (0.90)
  the two profiles are of different devices: /device:TPU:48 before, /device:TPU:32 now
where the time goes in v2:
time: 38.1 us; the launch traced here: 38 us
  Pallas kernels  36.4 us (96%)
  local copies, waits for them, and re-layouts  1.55 us (4%)
    pallas_call x1, Pallas kernels, on_device(): pl.pallas_call(functools.partial(kernel, row_count), out_shape=jax.ShapeD...  36.4 us
    unnamed x1, local copies, waits for them, and re-layouts  1.55 us

profile of v2, /device:TPU:32, one launch (start us, length us, event | category | flops | bytes accessed | tf_op | source)
XLA Modules:
  0.0 38.0 jit_solution(30193066578698114)
XLA Ops:
  0.0 36.4 %triple_product.1 = f32[7,32,128]{2,1,0:T(8,128)} custom-call(f32[64,32,128]{2,1,0:T(8,128)} %bitcast.10, s32[1,64]{1,0:T(1,128)} %bitcast.13, f32[64,64,128]{2,1,0:T(8,128)} %bitcast.9, s32[2,64]{1,0:T(2,128)} %bitcast.12, s32[64]{0:T(128)} %alen_any.1), custom_call_target="tpu_custom_call" | custom-call | tf_op jit(solution)/shard_map/triple_product/pallas_call | solution.py:412
  36.4 1.6 %copy.11 = f32[1,7,4096]{2,0,1:T(1,128)} copy(f32[1,7,4096]{2,0,1:T(1,128)} %bitcast.11) | data formatting | bytes 229376

commit v3 on v2

--- a/solution.py
+++ b/solution.py
@@ -67,6 +67,7 @@
     cross_recv_sem,
     sum_send_sem,
     sum_recv_sem,
+    last_send_sem,
 ):
     row = lax.axis_index("row")
     task = lax.axis_index("task")
@@ -114,22 +115,22 @@
 
     pl.semaphore_wait(barrier, jnp.where(has_edge, 8, 7))
 
+    halo_copy = pltpu.make_async_remote_copy(
+        p_hbm.at[pl.ds(58 * core, FW)], p_halo, halo_send_sem, halo_recv_sem, device_id=edge_id, device_id_type=MESH
+    )
+    pcol_copy = pltpu.make_async_remote_copy(
+        pcol_any, pcol_halo_v, int_send_sem.at[1], int_recv_sem.at[1], device_id=edge_id, device_id_type=MESH
+    )
+
+    @pl.when(has_edge)
+    def _():
+        halo_copy.start()
+        pcol_copy.start()
+
     acol_copy = pltpu.make_async_remote_copy(
         acol_any, acol_sib_v, int_send_sem.at[0], int_recv_sem.at[0], device_id=sib_id, device_id_type=MESH
     )
     acol_copy.start()
-    pcol_copy = pltpu.make_async_remote_copy(
-        pcol_any, pcol_halo_v, int_send_sem.at[1], int_recv_sem.at[1], device_id=edge_id, device_id_type=MESH
-    )
-    halo_copy = pltpu.make_async_remote_copy(
-        p_hbm.at[pl.ds(58 * core, FW)], p_halo, halo_send_sem, halo_recv_sem, device_id=edge_id, device_id_type=MESH
-    )
-
-    @pl.when(has_edge)
-    def _():
-        pcol_copy.start()
-        halo_copy.start()
-
     a_sends = []
     for u in range(4):
         copy = pltpu.make_async_remote_copy(
@@ -280,7 +281,7 @@
             flat.at[w],
             gathered.at[chip],
             sum_send_sem.at[w],
-            sum_recv_sem.at[chip],
+            sum_recv_sem.at[chip, 0],
             device_id=(row, owner),
             device_id_type=MESH,
         )
@@ -300,9 +301,37 @@
     sib_copy = pltpu.make_async_remote_copy(
         sib_out, sib_in, cross_send_sem.at[0], cross_recv_sem.at[0], device_id=sib_id, device_id_type=MESH
     )
-    edge_copy = pltpu.make_async_remote_copy(
-        edge_out, edge_in, cross_send_sem.at[1], cross_recv_sem.at[1], device_id=edge_id, device_id_type=MESH
-    )
+    edge_copies = [
+        pltpu.make_async_remote_copy(
+            edge_out.at[k],
+            edge_in.at[k],
+            cross_send_sem.at[1 + k],
+            cross_recv_sem.at[1 + k],
+            device_id=edge_id,
+            device_id_type=MESH,
+        )
+        for k in range(5)
+    ]
+
+    last_owner = home_of(3, core)
+    last_local = last_owner == task
+
+    def last_copy(k, source):
+        place = pl.ds(5 - 5 * core, 2) if k == 5 else pl.ds(2 * core + k, 1)
+        return pltpu.make_async_remote_copy(
+            flat.at[3, place],
+            gathered.at[source, place],
+            last_send_sem.at[k],
+            sum_recv_sem.at[source, k],
+            device_id=(row, last_owner),
+            device_id_type=MESH,
+        )
+
+    def send_last(k):
+        @pl.when(jnp.logical_not(last_local))
+        def _():
+            last_copy(k, chip).start()
+
     everything = range(-3, 4)
 
     def work(u):
@@ -338,7 +367,8 @@
         @pl.when(has_edge)
         def _():
             flatten(4, range(-3, 2), edge_out, 2 - 2 * core)
-            edge_copy.start()
+            for copy in edge_copies:
+                copy.start()
 
     work(0)
     flatten(-1, range(-1, 4), sib_out, 2 * core)
@@ -368,35 +398,53 @@
     send_sum(2)
     flatten(3, everything, flat.at[3], 0)
 
-    @pl.when(has_edge)
+    send_last(5)
+    for k in range(5):
+
+        @pl.when(has_edge)
+        def _():
+            edge_copies[k].wait()
+            flat[3, 2 * core + k] += edge_in[k]
+
+        send_last(k)
+
+    @pl.when(last_local)
     def _():
-        edge_copy.wait()
-        begin = 2 * core
-        for k in range(5):
-            flat[3, begin + k] += edge_in[k]
-
-    send_sum(3)
-
-    for w in range(4):
+        gathered[chip] = flat[3]
+
+    for w in range(3):
         copy, local = sum_copy(w)
 
         @pl.when(jnp.logical_not(local))
         def _():
             copy.wait_send()
 
+    @pl.when(jnp.logical_not(last_local))
+    def _():
+        for k in range(6):
+            last_copy(k, chip).wait_send()
+
+    owns_last = jnp.logical_or(task == 0, task == 7)
     for source in range(4):
         copy = pltpu.make_async_remote_copy(
             flat.at[0],
             gathered.at[source],
             sum_send_sem.at[0],
-            sum_recv_sem.at[source],
+            sum_recv_sem.at[source, 0],
             device_id=(row, other),
             device_id_type=MESH,
         )
 
-        @pl.when(jnp.logical_not(jnp.logical_and(mine, chip == source)))
+        elsewhere = jnp.logical_not(jnp.logical_and(mine, chip == source))
+
+        @pl.when(jnp.logical_and(elsewhere, jnp.logical_not(owns_last)))
         def _():
             copy.wait_recv()
+
+        @pl.when(jnp.logical_and(elsewhere, owns_last))
+        def _():
+            for k in range(6):
+                last_copy(k, source).wait_recv()
 
     out_ref[...] = (gathered[0] + gathered[1]) + (gathered[2] + gathered[3])
 
@@ -447,16 +495,17 @@
             pltpu.SMEM((1, SLAB), jnp.int32),
             pltpu.SMEM((SLAB,), jnp.int32),
             pltpu.SMEM((2, SLAB), jnp.int32),
-            dma((2,)),
-            dma((2,)),
-            dma((4,)),
-            dma((4,)),
+            dma((6,)),
+            dma((6,)),
+            dma((3,)),
+            dma((4, 6)),
+            dma((6,)),
         ],
         compiler_params=pltpu.CompilerParams(
-            collective_id=0, has_side_effects=True, vmem_limit_bytes=60 * 1024 * 1024
+            collective_id=0, has_side_effects=True, vmem_limit_bytes=40 * 1024 * 1024
         ),
         name="triple_product",
-    )(a_tiles, acol, p_tiles, pcol, alen)
+    )(*[pltpu.with_memory_space_constraint(x, pltpu.HBM) for x in (a_tiles, acol, p_tiles, pcol, alen)])
     return out.reshape(1, 7, TILE * TILE)
 
 

time: 38.1 us -> 36 us (0.945)
  Pallas kernels: 36.4 us -> 35.2 us
  local copies, waits for them, and re-layouts: 1.55 us -> 0.65 us
    pallas_call x1, Pallas kernels: 36.4 us -> 35.2 us  [on_device(): pl.pallas_call(functools.partial(kernel, row_count), out_shape=jax.ShapeD...]
    unnamed x1, local copies, waits for them, and re-layouts: 1.55 us -> 0.65 us
where the time goes in v3:
time: 36 us; the launch traced here: 35.9 us
  Pallas kernels  35.2 us (98%)
  local copies, waits for them, and re-layouts  0.65 us (2%)
    pallas_call x1, Pallas kernels, on_device(): pl.pallas_call(functools.partial(kernel, row_count), out_shape=jax.ShapeD...  35.2 us

profile of v3, /device:TPU:32, one launch (start us, length us, event | category | flops | bytes accessed | tf_op | source)
XLA Modules:
  0.0 35.9 jit_solution(15379268602216680261)
XLA Ops:
  0.0 35.2 %triple_product.1 = f32[7,32,128]{2,1,0:T(8,128)S(1)} custom-call(f32[64,32,128]{2,1,0:T(8,128)} %bitcast.11, s32[1,64]{1,0:T(1,128)} %bitcast.13, f32[64,64,128]{2,1,0:T(8,128)} %bitcast.10, s32[2,64]{1,0:T(2,128)} %bitcast.12, s32[64]{0:T(128)} %alen_any.1), custom_call_target="tpu_custom_call" | custom-call | tf_op jit(solution)/shard_map/triple_product/pallas_call | solution.py:460
  35.2 0.6 %copy.11 = f32[1,7,4096]{2,0,1:T(1,128)} copy(f32[1,7,4096]{2,0,1:T(1,128)S(1)} %bitcast.9) | data formatting | bytes 229376

commit v4 on v3

--- a/solution.py
+++ b/solution.py
@@ -42,6 +42,8 @@
     band_high,
     band_low,
     left,
+    stage_tiles,
+    stage_rows,
     ap_high,
     ap_low,
     sums,
@@ -201,24 +203,46 @@
 
         lax.fori_loop(0, count, one, 0, unroll=True)
 
-    def products(u):
+    def left_tile(tiles, slot, u, k):
+        live = jnp.where(slot < alen[8 * home_of(u, core) + k], 1.0, 0.0).astype(F32)
+        raw = tiles[8 * u + k] * live
+        near = jnp.take_along_axis(raw, parity_order, axis=1)
+        far = pltpu.roll(near, TILE, 1)
+        high, low = split(jnp.concatenate([jnp.where(lower, near, far), jnp.where(lower, far, near)], axis=0))
+        return jnp.concatenate([high, low[:, :TILE]], axis=1)
+
+    def left_rows(u):
+        high_parts, low_parts = [], []
+        for d in range(3):
+            high_row, low_row = [], []
+            for group in range(2):
+                high, low = split(left[u, d, group].T)
+                high_row += [high[:TILE], high[TILE:]]
+                low_row += [low[:TILE], low[TILE:]]
+            high_parts.append(jnp.concatenate(high_row, axis=1))
+            low_parts.append(jnp.concatenate(low_row, axis=1))
+        return jnp.concatenate(high_parts, axis=0), jnp.concatenate(low_parts, axis=0)
+
+    def stage(u):
+        def one(k, carry):
+            stage_tiles[2 * k] = left_tile(a_own, task, u, k)
+            stage_tiles[2 * k + 1] = left_tile(a_sib, other, u, k)
+            return carry
+
+        lax.fori_loop(0, 8, one, 0, unroll=True)
+        stage_rows[0], stage_rows[1] = left_rows(u)
+
+    def products(u, staged):
         home = home_of(u, core)
 
         def one(k, carry):
             j = 8 * home + k
-            length = alen[j]
             zero = jnp.zeros((TILE, 128), jnp.int32)
             total = [0.0, 0.0, 0.0]
-            for tiles, columns, slot in ((a_own, acol, task), (a_sib, acol_sib, other)):
+            for which, (tiles, columns, slot) in enumerate(((a_own, acol, task), (a_sib, acol_sib, other))):
                 column = columns[0, j] - SLAB * row
                 v = jnp.clip(31 - column + core * (2 * column - 63), -FW, HALF + FW - 1)
-                live = jnp.where(slot < length, 1.0, 0.0).astype(F32)
-                raw = tiles[8 * u + k] * live
-                near = jnp.take_along_axis(raw, parity_order, axis=1)
-                far = pltpu.roll(near, TILE, 1)
-                twice = jnp.concatenate([jnp.where(lower, near, far), jnp.where(lower, far, near)], axis=0)
-                high, low = split(twice)
-                tile = jnp.concatenate([high, low[:, :TILE]], axis=1)
+                tile = stage_tiles[2 * k + which] if staged else left_tile(tiles, slot, u, k)
                 right_high = band_high[v + FW]
                 right_low = band_low[v + FW]
                 right = jnp.concatenate([right_high, right_low, right_high], axis=0)
@@ -241,18 +265,8 @@
 
         lax.fori_loop(0, 8, one, 0, unroll=True)
 
-    def coarse(u):
-        high_parts, low_parts = [], []
-        for d in range(3):
-            high_row, low_row = [], []
-            for group in range(2):
-                high, low = split(left[u, d, group].T)
-                high_row += [high[:TILE], high[TILE:]]
-                low_row += [low[:TILE], low[TILE:]]
-            high_parts.append(jnp.concatenate(high_row, axis=1))
-            low_parts.append(jnp.concatenate(low_row, axis=1))
-        high = jnp.concatenate(high_parts, axis=0)
-        low = jnp.concatenate(low_parts, axis=0)
+    def coarse(u, staged):
+        high, low = (stage_rows[0], stage_rows[1]) if staged else left_rows(u)
         result = jnp.dot(high, ap_high[...], preferred_element_type=F32)
         result = result + jnp.dot(high, ap_low[...], preferred_element_type=F32)
         result = result + jnp.dot(low, ap_high[...], preferred_element_type=F32)
@@ -327,6 +341,25 @@
             device_id_type=MESH,
         )
 
+    next_owner = home_of(2, core)
+    next_local = next_owner == task
+
+    def next_copy(k, source):
+        place = pl.ds(5 - 5 * core, 2) if k == 1 else pl.ds(2 * core, 5)
+        return pltpu.make_async_remote_copy(
+            flat.at[2, place],
+            gathered.at[source, place],
+            sum_send_sem.at[2 + k],
+            sum_recv_sem.at[source, k],
+            device_id=(row, next_owner),
+            device_id_type=MESH,
+        )
+
+    def send_next(k):
+        @pl.when(jnp.logical_not(next_local))
+        def _():
+            next_copy(k, chip).start()
+
     def send_last(k):
         @pl.when(jnp.logical_not(last_local))
         def _():
@@ -335,10 +368,11 @@
     everything = range(-3, 4)
 
     def work(u):
-        a_copies[u].wait()
-        a_sends[u].wait()
-        products(u)
-        coarse(u)
+        if u < 3:
+            a_copies[u].wait()
+            a_sends[u].wait()
+        products(u, u == 3)
+        coarse(u, u == 3)
 
     for copy in int_copies:
         copy.wait()
@@ -353,6 +387,10 @@
     to_smem.wait()
 
     def edge_home():
+        a_copies[3].wait()
+        a_sends[3].wait()
+        stage(3)
+
         @pl.when(has_edge)
         def _():
             pcol_copy.wait()
@@ -390,12 +428,20 @@
     flatten(1, everything, flat.at[1], 0)
     send_sum(1)
 
+    flatten(2, (-3, -2), flat.at[2], 0)
+    send_next(1)
+
     @pl.when(core == 0)
     def _():
         edge_home()
 
-    flatten(2, everything, flat.at[2], 0)
-    send_sum(2)
+    flatten(2, range(-1, 4), flat.at[2], 0)
+    send_next(0)
+
+    @pl.when(next_local)
+    def _():
+        gathered[chip] = flat[2]
+
     flatten(3, everything, flat.at[3], 0)
 
     send_last(5)
@@ -412,7 +458,7 @@
     def _():
         gathered[chip] = flat[3]
 
-    for w in range(3):
+    for w in range(2):
         copy, local = sum_copy(w)
 
         @pl.when(jnp.logical_not(local))
@@ -424,7 +470,13 @@
         for k in range(6):
             last_copy(k, chip).wait_send()
 
+    @pl.when(jnp.logical_not(next_local))
+    def _():
+        for k in range(2):
+            next_copy(k, chip).wait_send()
+
     owns_last = jnp.logical_or(task == 0, task == 7)
+    owns_next = jnp.logical_or(task == 1, task == 6)
     for source in range(4):
         copy = pltpu.make_async_remote_copy(
             flat.at[0],
@@ -437,9 +489,14 @@
 
         elsewhere = jnp.logical_not(jnp.logical_and(mine, chip == source))
 
-        @pl.when(jnp.logical_and(elsewhere, jnp.logical_not(owns_last)))
+        @pl.when(jnp.logical_and(elsewhere, jnp.logical_not(jnp.logical_or(owns_last, owns_next))))
         def _():
             copy.wait_recv()
+
+        @pl.when(jnp.logical_and(elsewhere, owns_next))
+        def _():
+            for k in range(2):
+                next_copy(k, source).wait_recv()
 
         @pl.when(jnp.logical_and(elsewhere, owns_last))
         def _():
@@ -474,6 +531,8 @@
             pltpu.VMEM((44, TILE, 256), BF16),
             pltpu.VMEM((44, TILE, 256), BF16),
             pltpu.VMEM((4, 3, 2, 128, 128), F32),
+            pltpu.VMEM((16, TILE, 192), BF16),
+            pltpu.VMEM((2, 192, 512), BF16),
             pltpu.VMEM((512, 384), BF16),
             pltpu.VMEM((512, 384), BF16),
             pltpu.VMEM((6, 4, TILE, 128), F32),
@@ -497,7 +556,7 @@
             pltpu.SMEM((2, SLAB), jnp.int32),
             dma((6,)),
             dma((6,)),
-            dma((3,)),
+            dma((4,)),
             dma((4, 6)),
             dma((6,)),
         ],

time: 36 us -> 35.8 us (level)
  no operation moved by 1% of the time
where the time goes in v4:
time: 35.8 us; the launch traced here: 35.7 us
  Pallas kernels  35 us (98%)
  local copies, waits for them, and re-layouts  0.65 us (2%)
    pallas_call x1, Pallas kernels, on_device(): pl.pallas_call(functools.partial(kernel, row_count), out_shape=jax.ShapeD...  35 us

profile of v4, /device:TPU:32, one launch (start us, length us, event | category | flops | bytes accessed | tf_op | source)
XLA Modules:
  0.0 35.7 jit_solution(13312682449515499953)
XLA Ops:
  0.0 35.0 %triple_product.1 = f32[7,32,128]{2,1,0:T(8,128)S(1)} custom-call(f32[64,32,128]{2,1,0:T(8,128)} %bitcast.11, s32[1,64]{1,0:T(1,128)} %bitcast.13, f32[64,64,128]{2,1,0:T(8,128)} %bitcast.10, s32[2,64]{1,0:T(2,128)} %bitcast.12, s32[64]{0:T(128)} %alen_any.1), custom_call_target="tpu_custom_call" | custom-call | tf_op jit(solution)/shard_map/triple_product/pallas_call | solution.py:517
  35.0 0.6 %copy.11 = f32[1,7,4096]{2,0,1:T(1,128)} copy(f32[1,7,4096]{2,0,1:T(1,128)S(1)} %bitcast.9) | data formatting | bytes 229376
